TPU v7x, 128 devices: a whole 4x4x4 slice. The times are simulated.
128 devices in a mesh: row: 16 (over y, x), col: 8 (over z, core).
Axes of the slice: x: 4, y: 4, z: 4, core: 2. Of those that a mesh axis runs over, the one named last changes fastest.
Arguments:
- activations: bfloat16 [4096, 8192], P('row', 'col'), may hold values from -6 to 6
- out_grads: bfloat16 [4096, 8192], P('col', 'row'), may hold values from -6 to 6
- input_basis: bfloat16 [8192, 8192], P('col', 'row'), may hold values from -0.0625 to 0.0625
- output_basis: bfloat16 [8192, 8192], P('row', 'col'), may hold values from -0.0625 to 0.0625
Outputs:
- correction: float32 [8192, 8192], P('row', 'col')
All inputs are finite; a program needn't handle non-finite values.
Results may differ from a plain program's by a relative error of at most 0.02.
Values may be sent and summed in bfloat16 or wider, within the bound.
A program may use at most 128 MiB of HBM per device.

v0:
```python
import jax
import jax.numpy as jnp
from jax import lax
from jax.sharding import PartitionSpec as P

SEQS = 4
SEQ_LEN = 1024


def shards(activations, out_grads, input_basis, output_basis):
    act_part = jnp.dot(
        lax.all_gather(activations, "row", axis=0, tiled=True),
        input_basis,
        preferred_element_type=jnp.float32,
    ).astype(jnp.bfloat16)
    grad_part = jnp.dot(
        lax.all_gather(out_grads, "col", axis=0, tiled=True),
        output_basis,
        preferred_element_type=jnp.float32,
    ).astype(jnp.bfloat16)
    act_rot = lax.psum(act_part, "col").astype(jnp.float32).astype(jnp.bfloat16)
    grad_rot = lax.psum(grad_part, "row").astype(jnp.float32).astype(jnp.bfloat16)
    act_seqs = act_rot.reshape(SEQS, SEQ_LEN, act_rot.shape[1])
    grad_seqs = grad_rot.reshape(SEQS, SEQ_LEN, grad_rot.shape[1])
    tiles = jnp.einsum("nti,ntj->nij", act_seqs, grad_seqs, preferred_element_type=jnp.float32)
    return jnp.sum(tiles * tiles, axis=0) / (SEQS * SEQ_LEN)


def solution(mesh):
    return jax.shard_map(
        shards,
        mesh=mesh,
        in_specs=(P("row", "col"), P("col", "row"), P("col", "row"), P("row", "col")),
        out_specs=P("row", "col"),
        check_vma=False,
    )
```

profile of v0, /device:TPU:0, one launch (start us, length us, event | category | flops | bytes accessed | tf_op | source)
XLA Modules:
  0.0 353.0 jit_solution(16678369062752929964)
XLA Ops:
  6.5 0.0 copy-start
  6.5 0.0 all-gather.5.cloned.1.call-start
  6.5 0.7 all-gather.5.cloned.1.call-update
  7.3 0.0 all-gather.3.cloned.1.call-start
  7.3 0.7 all-gather.3.cloned.1.call-update
  8.0 0.0 all-reduce.5.cloned.1.call-start
  8.1 35.9 %all-gather.5.cloned.1.call-done = bf16[4096,512]{1,0:T(8,128)(2,1)} async-done(((bf16[512,512]{1,0:T(8,128)(2,1)}), bf16[4096,512]{1,0:T(8,128)(2,1)}) %all-gather.5.cloned.1.call-update) | async-done | bytes 4194320 | tf_op jit(solution)/shard_map/all_gather | solution.py:17
  43.9 0.0 copy-done
  43.9 8.9 %convolution_convert_fusion = bf16[4096,1024]{1,0:T(8,128)(2,1)} fusion(bf16[4096,512]{1,0:T(8,128)(2,1)} %all-gather.5.cloned.1.call-done, bf16[512,1024]{1,0:T(8,128)(2,1)S(1)} %copy-done), kind=kOutput, calls=%fused_computation.1 | convolution fusion | flops 4299161600 | bytes 13631488 | tf_op jit(solution)/shard_map/dot_general | solution.py:16
  52.8 0.0 copy-start.1
  52.8 0.0 all-reduce.5.cloned.1.call-update
  52.8 0.0 all-reduce.3.cloned.1.call-start
  52.9 63.6 %all-gather.3.cloned.1.call-done = bf16[4096,1024]{1,0:T(8,128)(2,1)} async-done(((bf16[256,1024]{1,0:T(8,128)(2,1)}), bf16[4096,1024]{1,0:T(8,128)(2,1)}) %all-gather.3.cloned.1.call-update) | async-done | bytes 8388624 | tf_op jit(solution)/shard_map/all_gather | solution.py:12
  116.5 0.0 copy-done.1
  116.5 9.5 %convolution_convert_fusion.1 = bf16[4096,512]{1,0:T(8,128)(2,1)} fusion(bf16[4096,1024]{1,0:T(8,128)(2,1)} %all-gather.3.cloned.1.call-done, bf16[1024,512]{1,0:T(8,128)(2,1)S(1)} %copy-done.1), kind=kOutput, calls=%fused_computation.2 | convolution fusion | flops 4297064448 | bytes 13631488 | tf_op jit(solution)/shard_map/dot_general | solution.py:11
  126.0 6.4 %copy.5 = bf16[4,1024,512]{1,2,0:T(8,128)(2,1)} copy(bf16[4,1024,512]{2,1,0:T(8,128)(2,1)} %bitcast.9) | data formatting | bytes 8388608 | tf_op jit(solution)/shard_map/reshape | solution.py:23
  132.4 0.0 all-reduce.3.cloned.1.call-update
  132.4 128.7 %all-reduce.5.cloned.1.call-done = bf16[4,1024,1024]{2,1,0:T(8,128)(2,1)} async-done(((bf16[4,1024,1024]{2,1,0:T(8,128)(2,1)}), bf16[4,1024,1024]{2,1,0:T(8,128)(2,1)}) %all-reduce.5.cloned.1.call-update) | async-done | bytes 8388624 | tf_op jit(solution)/shard_map/psum | solution.py:22
  261.1 74.3 %all-reduce.3.cloned.1.call-done = bf16[4,1024,512]{1,2,0:T(8,128)(2,1)} async-done(((bf16[4,1024,512]{1,2,0:T(8,128)(2,1)}), bf16[4,1024,512]{1,2,0:T(8,128)(2,1)}) %all-reduce.3.cloned.1.call-update) | async-done | bytes 4194320 | tf_op jit(solution)/shard_map/psum | solution.py:21
  335.4 9.4 %multiply_reduce_fusion = f32[512,1024]{1,0:T(8,128)S(1)} fusion(bf16[4,1024,512]{1,2,0:T(8,128)(2,1)} %all-reduce.3.cloned.1.call-done, bf16[4,1024,1024]{2,1,0:T(8,128)(2,1)} %all-reduce.5.cloned.1.call-done), kind=kOutput, calls=%fused_computation | convolution fusion | flops 4298637312 | bytes 14680064 | tf_op jit(solution)/shard_map/nti,ntj->nij/dot_general | solution.py:25
  344.8 1.6 broadcast_multiply_fusion
Async XLA Ops:
  6.5 37.4 %copy-start = (bf16[512,1024]{1,0:T(8,128)(2,1)S(1)}, bf16[512,1024]{1,0:T(8,128)(2,1)}, u32[]{:S(2)}) copy-start(bf16[512,1024]{1,0:T(8,128)(2,1)} %param.7) | copy-start | bytes 3145732
  6.5 37.4 %all-gather.5.cloned.1.call-start = ((), (), s32[]{:S(2)}) async-start(), calls=%async_computation.2 | async-start | bytes 4718592 | tf_op jit(solution)/shard_map/all_gather | solution.py:17
  7.3 109.2 %all-gather.3.cloned.1.call-start = ((), (), s32[]{:S(2)}) async-start(), calls=%async_computation | async-start | bytes 8912896 | tf_op jit(solution)/shard_map/all_gather | solution.py:12
  8.0 253.1 %all-reduce.5.cloned.1.call-start = ((), (), s32[]{:S(2)}) async-start(), calls=%async_computation.3 | async-start | bytes 16777216 | tf_op jit(solution)/shard_map/psum | solution.py:22
  52.8 63.7 %copy-start.1 = (bf16[1024,512]{1,0:T(8,128)(2,1)S(1)}, bf16[1024,512]{1,0:T(8,128)(2,1)}, u32[]{:S(2)}) copy-start(bf16[1024,512]{1,0:T(8,128)(2,1)} %param.6) | copy-start | bytes 3145732
  52.8 282.6 %all-reduce.3.cloned.1.call-start = ((), (), s32[]{:S(2)}) async-start(), calls=%async_computation.1 | async-start | bytes 8388608 | tf_op jit(solution)/shard_map/psum | solution.py:21
Sparse Core Ops, SparseCore 0:
  9.1 34.7 all-gather.4
  46.0 70.4 all-gather.2
  120.1 140.9 all-reduce.4
  263.5 71.9 all-reduce.2
where the time goes:
time: 353 us
  waiting for transfers between devices  304 us (86%)
  matrix products  27.8 us (8%)
  between operations  13.1 us (4%)
  local copies, waits for them, and re-layouts  6.4 us (2%)
    psum x1, waiting for transfers between devices, shards(): lax.psum(grad_part, 'row').astype(jnp.float32).astype(jnp.bfloat16)  129 us
    psum x1, waiting for transfers between devices, shards(): act_rot = lax.psum(act_part, 'col').astype(jnp.float32).astype(jnp.bfloat16)  74.3 us
    all_gather x1, waiting for transfers between devices, shards(): lax.all_gather(activations, 'row', axis=0, tiled=True)  63.6 us
    all_gather x1, waiting for transfers between devices, shards(): lax.all_gather(out_grads, 'col', axis=0, tiled=True)  35.9 us
    dot_general x1, matrix products, shards(): jnp.dot(lax.all_gather(activations, 'row', axis=0, tiled=True), input_bas...  9.48 us
    dot_general x1, matrix products, shards(): jnp.einsum('nti,ntj->nij', act_seqs, grad_seqs, preferred_element_type=jn...  9.4 us
    dot_general x1, matrix products, shards(): jnp.dot(lax.all_gather(out_grads, 'col', axis=0, tiled=True), output_basi...  8.91 us
  transfers between devices with their start and end apart: 4, of which 4 were waited for; matrix products, arithmetic and copies ran while one was open for 7% of the time, Pallas kernels for 0%

commit v1 on v0

v1 whole, which is shorter than its diff:
```python
import functools

import jax
import jax.numpy as jnp
from jax import lax
from jax.experimental import pallas as pl
from jax.experimental.pallas import tpu as pltpu
from jax.sharding import PartitionSpec as P

SEQS = 4
SEQ_LEN = 1024
MESH = pl.DeviceIdType.MESH
BF16 = jnp.bfloat16
F32 = jnp.float32
N_SEM = 200


def at_multiple(index, size, step=None):
    return pl.ds(pl.multiple_of(index * (step or size), step or size), size)


def kernel(
    a_ref, g_ref, u_ref, v_ref, o_ref,
    a_all, u_all, g_all, v_all,
    act_out, act_in, act_part, act_s1, act_r1, act_s2, act_r2, act_t,
    grad_part, grad_s1, grad_r1, grad_s2, grad_r2, grad_rot,
    tile_part, tile_s1, tile_r1, tile_s2, tile_r2,
    send_sem, recv_sem, local_sem,
):
    row, col = lax.axis_index("row"), lax.axis_index("col")
    y, x = lax.div(row, 4), lax.rem(row, 4)
    z, core = lax.div(col, 2), lax.rem(col, 2)
    mate = 1 - core

    def step(position, by):
        return lax.rem(position + by, 4)

    def device(y, x, z, core):
        return (y * 4 + x, z * 2 + core)

    x_ring = (device(y, step(x, 1), z, core), device(y, step(x, 3), z, core))
    y_ring = (device(step(y, 1), x, z, core), device(step(y, 3), x, z, core))
    z_ring = (device(y, x, step(z, 1), core), device(y, x, step(z, 3), core))
    x_far = device(y, step(x, 2), z, core)
    other = device(y, x, z, mate)

    partners = (*x_ring, *y_ring, *z_ring, x_far, other)
    barrier = pltpu.get_barrier_semaphore()
    for partner in partners:
        pl.semaphore_signal(barrier, inc=1, device_id=partner, device_id_type=MESH)
    pl.semaphore_wait(barrier, len(partners))

    sent = []

    def send(src, dst, target):
        index = len(sent)
        copy = pltpu.make_async_remote_copy(
            src_ref=src, dst_ref=dst,
            send_sem=send_sem.at[index], recv_sem=recv_sem.at[index],
            device_id=target, device_id_type=MESH,
        )
        copy.start()
        sent.append(copy)
        return copy

    local = []

    def keep(src, dst):
        copy = pltpu.make_async_copy(src, dst, local_sem.at[len(local)])
        copy.start()
        local.append(copy)
        return copy

    class Gather:
        def __init__(self, slot, position, ring, own=None):
            own = own or (lambda half: slot(position, half))
            self.slot, self.position, self.ring = slot, position, ring
            right, left = ring
            self.r0 = send(own(0), slot(position, 0), right)
            self.l1 = send(own(1), slot(position, 1), left)
            self.r1 = send(own(1), slot(position, 1), right)
            self.l0 = send(own(0), slot(position, 0), left)

        def forward(self):
            right, left = self.ring
            self.r0.wait_recv()
            before = self.slot(step(self.position, 3), 0)
            self.rr = send(before, before, right)
            self.l1.wait_recv()
            after = self.slot(step(self.position, 1), 1)
            self.ll = send(after, after, left)

        def near(self):
            self.r1.wait_recv()
            self.l0.wait_recv()

        def far(self):
            self.rr.wait_recv()
            self.ll.wait_recv()

    class Reduce:
        def __init__(self, part, half, position, ring, s1, r1, s2, r2):
            self.part, self.half, self.position, self.ring = part, half, position, ring
            self.s1, self.r1, self.s2, self.r2 = s1, r1, s2, r2

        def first(self):
            right, left = self.ring
            block = self.part(step(self.position, 2))
            self.s1[0] = block[:self.half].astype(BF16)
            self.s1[1] = block[self.half:].astype(BF16)
            self.right1 = send(self.s1.at[0], self.r1.at[0], right)
            self.left1 = send(self.s1.at[1], self.r1.at[1], left)

        def second(self):
            right, left = self.ring
            half = self.half
            block = self.part(step(self.position, 1))
            self.right1.wait_recv()
            self.s2[0, :half] = (block[:half] + self.r1[0].astype(F32)).astype(BF16)
            self.s2[0, half:] = block[half:].astype(BF16)
            self.right2 = send(self.s2.at[0], self.r2.at[0], right)
            block = self.part(step(self.position, 3))
            self.left1.wait_recv()
            self.s2[1, :half] = block[:half].astype(BF16)
            self.s2[1, half:] = (block[half:] + self.r1[1].astype(F32)).astype(BF16)
            self.left2 = send(self.s2.at[1], self.r2.at[1], left)

        def last(self):
            block = self.part(self.position)
            self.right2.wait_recv()
            self.left2.wait_recv()
            return block + self.r2[0].astype(F32) + self.r2[1].astype(F32)

    own_rows = pl.multiple_of(z * 256 + core * 128, 128)
    lanes = at_multiple(x, 512)
    swaps = []
    for by, target in ((1, x_ring[0]), (3, x_ring[1]), (2, x_far)):
        swaps.append(send(
            g_ref.at[at_multiple(step(x, by), 128)],
            g_all.at[pl.ds(own_rows, 128), lanes], target))
    g_own = keep(g_ref.at[at_multiple(x, 128)], g_all.at[pl.ds(own_rows, 128), lanes])

    u_gather = Gather(
        lambda p, half: u_all.at[p * 2 + half], y, y_ring,
        own=lambda half: u_ref.at[:, pl.ds(half * 256, 256)])
    a_gather = Gather(
        lambda p, half: a_all.at[pl.ds(pl.multiple_of(p * 256 + half * 128, 128), 128)], x, x_ring,
        own=lambda half: a_ref.at[pl.ds(half * 128, 128)])
    keeps = [
        keep(a_ref, a_all.at[at_multiple(x, 256)]),
        keep(u_ref.at[:, pl.ds(0, 256)], u_all.at[y * 2]),
        keep(u_ref.at[:, pl.ds(256, 256)], u_all.at[y * 2 + 1]),
    ]
    for c in range(4):
        keeps.append(keep(v_ref.at[:, pl.ds(c * 256, 256)], v_all.at[c, at_multiple(x, 512)]))

    def v_start(c):
        return Gather(
            lambda p, half: v_all.at[c, pl.ds(pl.multiple_of(p * 512 + half * 256, 256), 256)], x, x_ring,
            own=lambda half: v_ref.at[pl.ds(half * 256, 256), pl.ds(c * 256, 256)])

    g_own.wait()
    for swap in swaps:
        swap.wait_recv()

    def g_rows(p, owner):
        return g_all.at[pl.ds(pl.multiple_of(p * 256 + owner * 128, 128), 128)]

    g_gather = Gather(
        lambda p, half: g_all.at[pl.ds(pl.multiple_of(p * 256 + core * 128 + half * 64, 64), 64)], z, z_ring)
    g_mates = [send(g_rows(z, core), g_rows(z, core), other)]

    a_gather.forward()
    v_gathers = [v_start(0)]
    g_gather.forward()
    u_gather.forward()
    v_gathers.append(v_start(1))
    for copy in keeps:
        copy.wait()
    a_gather.near()
    a_gather.far()

    def dot(a, b):
        return jnp.dot(a, b, preferred_element_type=F32)

    act_pieces = []

    class Piece:
        def __init__(self, s, block):
            self.s, self.block = s, block

            @pl.loop(0, 2)
            def _(m):
                rows = at_multiple(m, 512)
                act_out[s, rows] = dot(a_all[rows], u_all[block * 2 + mate]).astype(BF16)

            self.swap = send(act_out.at[s], act_in.at[s], other)

            @pl.loop(0, 2)
            def _(m):
                rows = at_multiple(m, 512)
                act_part[s, rows] = dot(a_all[rows], u_all[block * 2 + core])

            def part(t):
                rows = at_multiple(t, 256)
                return act_part[s, rows] + act_in[s, rows].astype(F32)

            self.reduce = Reduce(part, 128, z, z_ring, act_s1.at[s], act_r1.at[s], act_s2.at[s], act_r2.at[s])
            self.swap.wait_recv()
            self.reduce.first()

        def gather(self):
            total = self.reduce.last()
            rows = pl.multiple_of(self.block * 512 + core * 256, 256)
            act_t[pl.ds(rows, 256), at_multiple(z, 256)] = total.T.astype(BF16)
            self.gathered = Gather(
                lambda p, half: act_t.at[pl.ds(pl.multiple_of(rows + half * 128, 128), 128), at_multiple(p, 256)],
                z, z_ring)

        def finish(self):
            self.gathered.near()
            self.gathered.far()
            rows = pl.multiple_of(self.block * 512 + core * 256, 256)
            piece = act_t.at[pl.ds(rows, 256)]
            self.mate = send(piece, piece, other)

    class Chunk:
        def __init__(self, c):
            self.c = c

            @pl.loop(0, 2)
            def _(m):
                rows = at_multiple(m, 512)
                grad_part[c, rows] = dot(g_all[rows], v_all[c])

            def part(t):
                return grad_part[c, at_multiple(t, 256)]

            self.reduce = Reduce(part, 128, y, y_ring, grad_s1.at[c], grad_r1.at[c], grad_s2.at[c], grad_r2.at[c])
            self.reduce.first()

        def gather(self):
            c = self.c
            total = self.reduce.last().astype(BF16)
            rows = at_multiple(x, 128)
            grad_rot[c, 0, rows] = total[:128]
            grad_rot[c, 1, rows] = total[128:]
            self.gathered = Gather(
                lambda p, half: grad_rot.at[c, half, at_multiple(p, 128)], x, x_ring)

        def finish(self):
            self.gathered.near()
            self.gathered.far()

        def tiles(self):
            c = self.c
            grads = grad_rot[c].reshape(1024, 256)

            def tile(t):
                product = dot(act_t[at_multiple(t, 512)], grads)
                return product * product

            def part(t):
                return tile(t)

            self.out = Reduce(part, 256, y, y_ring, tile_s1.at[c], tile_r1.at[c], tile_s2.at[c], tile_r2.at[c])
            self.out.first()

        def total(self):
            o_ref[:, pl.ds(self.c * 256, 256)] = self.out.last() * (1.0 / (SEQS * SEQ_LEN))

    pieces = [Piece(0, y)]
    u_gather.near()
    v_gathers[0].forward()
    g_gather.near()
    for by in (1, 3):
        g_mates.append(send(g_rows(step(z, by), core), g_rows(step(z, by), core), other))
    v_gathers.append(v_start(2))
    pieces.append(Piece(1, step(y, 3)))
    pieces[0].reduce.second()
    pieces.append(Piece(2, step(y, 1)))
    pieces[1].reduce.second()
    v_gathers[1].forward()
    g_gather.far()
    g_mates.append(send(g_rows(step(z, 2), core), g_rows(step(z, 2), core), other))
    v_gathers.append(v_start(3))
    pieces[2].reduce.second()
    pieces[0].gather()
    for copy in g_mates:
        copy.wait_recv()
    chunks = []
    v_gathers[0].near()
    v_gathers[0].far()
    chunks.append(Chunk(0))
    u_gather.far()
    pieces.append(Piece(3, step(y, 2)))
    pieces[0].gathered.forward()
    pieces[1].gather()
    chunks[0].reduce.second()
    pieces[3].reduce.second()
    v_gathers[2].forward()
    pieces[1].gathered.forward()
    pieces[2].gather()
    v_gathers[1].near()
    v_gathers[1].far()
    chunks.append(Chunk(1))
    chunks[0].gather()
    pieces[0].finish()
    pieces[2].gathered.forward()
    pieces[3].gather()
    chunks[1].reduce.second()
    chunks[0].gathered.forward()
    v_gathers[3].forward()
    pieces[1].finish()
    pieces[3].gathered.forward()
    v_gathers[2].near()
    v_gathers[2].far()
    chunks.append(Chunk(2))
    chunks[1].gather()
    pieces[2].finish()
    chunks[2].reduce.second()
    chunks[1].gathered.forward()
    v_gathers[3].near()
    v_gathers[3].far()
    chunks.append(Chunk(3))
    chunks[2].gather()
    pieces[3].finish()
    chunks[3].reduce.second()
    for piece in pieces:
        piece.mate.wait_recv()
    chunks[0].finish()
    chunks[0].tiles()
    chunks[2].gathered.forward()
    chunks[3].gather()
    chunks[1].finish()
    chunks[1].tiles()
    chunks[0].out.second()
    chunks[3].gathered.forward()
    chunks[2].finish()
    chunks[2].tiles()
    chunks[1].out.second()
    chunks[3].finish()
    chunks[3].tiles()
    chunks[2].out.second()
    chunks[0].total()
    chunks[3].out.second()
    chunks[1].total()
    chunks[2].total()
    chunks[3].total()
    for copy in sent:
        copy.wait_send()


def shards(activations, out_grads, input_basis, output_basis):
    vmem = pl.BlockSpec(memory_space=pltpu.VMEM)
    bf16_sizes = lambda *s: pltpu.VMEM(s, BF16)
    f32_sizes = lambda *s: pltpu.VMEM(s, F32)
    return pl.pallas_call(
        kernel,
        out_shape=jax.ShapeDtypeStruct((512, 1024), F32),
        in_specs=[vmem] * 4,
        out_specs=vmem,
        scratch_shapes=[
            bf16_sizes(1024, 1024), bf16_sizes(8, 1024, 256), bf16_sizes(1024, 2048), bf16_sizes(4, 2048, 256),
            bf16_sizes(4, 1024, 256), bf16_sizes(4, 1024, 256), f32_sizes(4, 1024, 256),
            bf16_sizes(4, 2, 128, 256), bf16_sizes(4, 2, 128, 256),
            bf16_sizes(4, 2, 256, 256), bf16_sizes(4, 2, 256, 256), bf16_sizes(2048, 1024),
            f32_sizes(4, 1024, 256),
            bf16_sizes(4, 2, 128, 256), bf16_sizes(4, 2, 128, 256),
            bf16_sizes(4, 2, 256, 256), bf16_sizes(4, 2, 256, 256), bf16_sizes(4, 2, 512, 256),
            f32_sizes(8, 128),
            bf16_sizes(4, 2, 256, 256), bf16_sizes(4, 2, 256, 256),
            bf16_sizes(4, 2, 512, 256), bf16_sizes(4, 2, 512, 256),
            pltpu.SemaphoreType.DMA((N_SEM,)), pltpu.SemaphoreType.DMA((N_SEM,)),
            pltpu.SemaphoreType.DMA((16,)),
        ],
        compiler_params=pltpu.CompilerParams(
            collective_id=0, has_side_effects=True, vmem_limit_bytes=60 * 2**20),
        cost_estimate=pl.CostEstimate(flops=13 * 10**9, bytes_accessed=5 * 2**20, transcendentals=0),
    )(activations, out_grads, input_basis, output_basis)


def solution(mesh):
    return jax.shard_map(
        shards,
        mesh=mesh,
        in_specs=(P("row", "col"), P("col", "row"), P("col", "row"), P("row", "col")),
        out_specs=P("row", "col"),
        check_vma=False,
    )
```

time: 353 us -> 132 us (0.37)
  waiting for transfers between devices: 304 us -> 0 us
  Pallas kernels: 0 us -> 129 us
  matrix products: 27.8 us -> 0 us
  between operations: 13.1 us -> 0.01 us
    psum x2 -> x0, waiting for transfers between devices: 203 us -> none  [the longest x1 129 us: shards(): lax.psum(grad_part, 'row').astype(jnp.float32).astype(jnp.bfloat16)]
    pallas_call x0 -> x1, Pallas kernels: none -> 129 us  [shards(): pl.pallas_call(kernel, out_shape=jax.ShapeDtypeStruct((512, 1024), F32),...]
    all_gather x2 -> x0, waiting for transfers between devices: 99.5 us -> none  [the longest x1 63.6 us: shards(): lax.all_gather(activations, 'row', axis=0, tiled=True)]
    dot_general x3 -> x0, matrix products: 27.8 us -> none  [the longest x1 9.48 us: shards(): jnp.dot(lax.all_gather(activations, 'row', axis=0, tiled=True), input_bas...]
    reshape x1 -> x0, local copies, waits for them, and re-layouts: 6.39 us -> none  [shards(): act_seqs = act_rot.reshape(SEQS, SEQ_LEN, act_rot.shape[1])]
  transfers between devices with their start and end apart: 4 -> 0, of which waited for: 4 -> 0; matrix products, arithmetic and copies ran while one was open for 7% -> 0% of each run, Pallas kernels for 0% -> 0%
where the time goes in v1:
time: 132 us
  Pallas kernels  129 us (98%)
  local copies, waits for them, and re-layouts  3.16 us (2%)
    pallas_call x1, Pallas kernels, shards(): pl.pallas_call(kernel, out_shape=jax.ShapeDtypeStruct((512, 1024), F32),...  129 us
    unnamed x1, local copies, waits for them, and re-layouts  3.16 us

profile of v1, /device:TPU:0, one launch (start us, length us, event | category | flops | bytes accessed | tf_op | source)
XLA Modules:
  0.0 131.7 jit_solution(17659013657098995418)
XLA Ops:
  0.0 128.5 %shard_map.46 = f32[512,1024]{1,0:T(8,128)} custom-call(bf16[256,1024]{1,0:T(8,128)(2,1)} %a_ref.1, bf16[512,512]{1,0:T(8,128)(2,1)} %g_ref.1, bf16[1024,512]{1,0:T(8,128)(2,1)} %u_ref.1, bf16[512,1024]{1,0:T(8,128)(2,1)} %v_ref.1), custom_call_target="tpu_custom_call" | custom-call | flops 12999999488 | bytes 5242880 | tf_op jit(solution)/shard_map/pallas_call | solution.py:358
  128.5 3.2 %copy.6 = f32[512,1024]{1,0:T(8,128)} copy(f32[512,1024]{1,0:T(8,128)} %shard_map.46) | data formatting | bytes 4194304

commit v2 on v0

v2 whole, which is shorter than its diff:
```python
import jax
import jax.numpy as jnp
from jax import lax
from jax.experimental import pallas as pl
from jax.experimental.pallas import tpu as pltpu
from jax.sharding import PartitionSpec as P

SEQS = 4
SEQ_LEN = 1024
MESH = pl.DeviceIdType.MESH
BF16 = jnp.bfloat16
F32 = jnp.float32
CHUNKS = 4
WIDTH = 1024 // CHUNKS
N_SEM = 120 + 24 * CHUNKS

ORDER = (
    "ga", "a.own1", "a.own2", "u.own1", "gk.own", "g.own1", "u.fwd", "a.fwd", "g.fwd", "v1.own1", "u.own2",
    "v2.own1", "g.own2", "v1.own2", "p1.own", "p1.out", "p0.out", "v1.fwd", "p2.out", "p1.r1", "p0.own",
    "p0.r1", "p2.own", "v3.own1", "v2.fwd", "v2.own2", "gk.near", "v0.own1", "p2.r1", "p1.r2", "p0.r2",
    "gk.far", "c1.mm", "v3.fwd", "p2.r2", "p3.out", "p1.own1", "p3.own", "v3.own2", "p3.r1", "c1.r2", "p0.own1",
    "c2.mm", "p2.own1", "p1.fwd", "p3.r2", "v0.fwd", "c1.own1", "c2.r2", "p2.fwd", "v0.own2", "p2.own2",
    "c3.mm", "p1.own2", "p3.own1", "p3.own2", "c1.own2", "c1.fwd", "c2.own1", "p0.fwd", "c3.r2", "p2.km",
    "c0.mm", "p3.fwd", "c2.own2", "c1.t1", "p0.own2", "c2.fwd", "c0.r2", "p1.km", "p3.km", "c3.own1", "c2.t1",
    "c3.own2", "c1.tn", "p0.km", "c1.t2", "c2.tn", "c3.fwd", "c0.own1", "c2.to", "c3.t1", "c0.fwd", "c0.own2",
    "c3.tn", "c2.t2", "c1.to", "c3.to", "c0.t1", "c0.to", "c1.fin", "c3.t2", "c0.tn", "c2.fin", "c0.t2",
    "c3.fin", "c0.fin",
)


def at_multiple(index, size, step=None):
    return pl.ds(pl.multiple_of(index * (step or size), step or size), size)


def dot(a, b):
    return jnp.dot(a, b, preferred_element_type=F32)


def kernel(
    a_ref, g_ref, u_ref, v_ref, o_ref,
    a_all, u_all, g_all, v_all,
    act_out, act_in, act_part, act_s1, act_r1, act_s2, act_r2, act_t,
    grad_part, grad_s1, grad_r1, grad_s2, grad_r2, grad_rot,
    tile_part, tile_s1, tile_r1, tile_s2, tile_r2,
    send_sem, recv_sem, local_sem,
):
    row, col = lax.axis_index("row"), lax.axis_index("col")
    y, x = lax.div(row, 4), lax.rem(row, 4)
    z, core = lax.div(col, 2), lax.rem(col, 2)
    mate = 1 - core

    def step(position, by):
        return lax.rem(position + by, 4)

    def device(y, x, z, core):
        return (y * 4 + x, z * 2 + core)

    x_ring = (device(y, step(x, 1), z, core), device(y, step(x, 3), z, core))
    y_ring = (device(step(y, 1), x, z, core), device(step(y, 3), x, z, core))
    z_ring = (device(y, x, step(z, 1), core), device(y, x, step(z, 3), core))
    x_far = device(y, step(x, 2), z, core)
    other = device(y, x, z, mate)

    local = []

    def keep(src, dst):
        copy = pltpu.make_async_copy(src, dst, local_sem.at[len(local)])
        copy.start()
        local.append(copy)
        return copy

    own_rows = pl.multiple_of(z * 256 + core * 128, 128)
    x_lanes = at_multiple(x, 512)
    g_keep = keep(g_ref.at[at_multiple(x, 128)], g_all.at[pl.ds(own_rows, 128), x_lanes])
    act_keeps = [
        keep(a_ref, a_all.at[at_multiple(x, 256)]),
        keep(u_ref.at[:, pl.ds(0, 256)], u_all.at[y * 2]),
        keep(u_ref.at[:, pl.ds(256, 256)], u_all.at[y * 2 + 1]),
    ]
    v_keeps = [
        keep(v_ref.at[:, pl.ds(c * WIDTH, WIDTH)], v_all.at[c, at_multiple(x, 512)]) for c in range(CHUNKS)
    ]

    partners = (*x_ring, *y_ring, *z_ring, x_far, other)
    barrier = pltpu.get_barrier_semaphore()
    for partner in partners:
        pl.semaphore_signal(barrier, inc=1, device_id=partner, device_id_type=MESH)
    pl.semaphore_wait(barrier, len(partners))

    sent, arrived = [], set()

    def send(src, dst, target):
        index = len(sent)
        copy = pltpu.make_async_remote_copy(
            src_ref=src, dst_ref=dst,
            send_sem=send_sem.at[index], recv_sem=recv_sem.at[index],
            device_id=target, device_id_type=MESH,
        )
        copy.start()
        sent.append(copy)
        return copy

    def arrive(*copies):
        for copy in copies:
            if id(copy) not in arrived:
                arrived.add(id(copy))
                copy.wait_recv()

    def landed(*copies):
        for copy in copies:
            if id(copy) not in arrived:
                arrived.add(id(copy))
                copy.wait()

    steps = {}

    class Gather:
        def __init__(self, name, slot, position, ring, own=None, ready=lambda: None):
            self.own = own or (lambda half: slot(position, half))
            self.slot, self.position, self.ring, self.ready = slot, position, ring, ready
            steps[name + ".own1"] = self.first
            steps[name + ".own2"] = self.second
            steps[name + ".fwd"] = self.forward

        def first(self):
            self.ready()
            right, left = self.ring
            self.r0 = send(self.own(0), self.slot(self.position, 0), right)
            self.l1 = send(self.own(1), self.slot(self.position, 1), left)

        def second(self):
            right, left = self.ring
            self.r1 = send(self.own(1), self.slot(self.position, 1), right)
            self.l0 = send(self.own(0), self.slot(self.position, 0), left)

        def forward(self):
            right, left = self.ring
            arrive(self.r0)
            before = self.slot(step(self.position, 3), 0)
            self.rr = send(before, before, right)
            arrive(self.l1)
            after = self.slot(step(self.position, 1), 1)
            self.ll = send(after, after, left)

        def early(self):
            arrive(self.r0, self.l1)

        def near(self):
            arrive(self.r0, self.l1, self.r1, self.l0)

        def far(self):
            arrive(self.rr, self.ll)

    class Reduce:
        def __init__(self, part, half, ring, s1, r1, s2, r2):
            self.part, self.half, self.ring = part, half, ring
            self.s1, self.r1, self.s2, self.r2 = s1, r1, s2, r2

        def first(self):
            right, left = self.ring
            block = self.part(2)
            self.s1[0] = block[:self.half].astype(BF16)
            self.s1[1] = block[self.half:].astype(BF16)
            self.right1 = send(self.s1.at[0], self.r1.at[0], right)
            self.left1 = send(self.s1.at[1], self.r1.at[1], left)

        def second(self):
            right, left = self.ring
            half = self.half
            block = self.part(1)
            arrive(self.right1)
            self.s2[0, :half] = (block[:half] + self.r1[0].astype(F32)).astype(BF16)
            self.s2[0, half:] = block[half:].astype(BF16)
            self.right2 = send(self.s2.at[0], self.r2.at[0], right)
            block = self.part(3)
            arrive(self.left1)
            self.s2[1, :half] = block[:half].astype(BF16)
            self.s2[1, half:] = (block[half:] + self.r1[1].astype(F32)).astype(BF16)
            self.left2 = send(self.s2.at[1], self.r2.at[1], left)

        def last(self):
            block = self.part(0)
            arrive(self.right2, self.left2)
            return block + self.r2[0].astype(F32) + self.r2[1].astype(F32)

    swaps = []

    def g_swap():
        for by, target in ((1, x_ring[0]), (3, x_ring[1]), (2, x_far)):
            swaps.append(send(
                g_ref.at[at_multiple(step(x, by), 128)],
                g_all.at[pl.ds(own_rows, 128), x_lanes], target))

    def g_swapped():
        landed(g_keep)
        arrive(*swaps)

    steps["ga"] = g_swap
    g_gather = Gather(
        "g", lambda p, half: g_all.at[pl.ds(pl.multiple_of(p * 256 + core * 128 + half * 64, 64), 64)],
        z, z_ring, ready=g_swapped)
    g_mates = []

    def g_mate(*offsets):
        for by in offsets:
            block = g_all.at[pl.ds(pl.multiple_of(step(z, by) * 256 + core * 128, 128), 128)]
            g_mates.append(send(block, block, other))

    def g_mate_own():
        g_swapped()
        g_mate(0)

    def g_mate_near():
        g_gather.near()
        g_mate(1, 3)

    def g_mate_far():
        g_gather.far()
        g_mate(2)

    steps["gk.own"], steps["gk.near"], steps["gk.far"] = g_mate_own, g_mate_near, g_mate_far

    def g_done():
        g_gather.near()
        g_gather.far()
        arrive(*g_mates)

    u_gather = Gather(
        "u", lambda p, half: u_all.at[p * 2 + half], y, y_ring,
        own=lambda half: u_ref.at[:, pl.ds(half * 256, 256)])
    a_gather = Gather(
        "a", lambda p, half: a_all.at[pl.ds(pl.multiple_of(p * 256 + half * 128, 128), 128)], x, x_ring,
        own=lambda half: a_ref.at[pl.ds(half * 128, 128)])
    v_gathers = [
        Gather(
            f"v{c}",
            lambda p, half, c=c: v_all.at[c, pl.ds(pl.multiple_of(p * 512 + half * 256, 256), 256)], x, x_ring,
            own=lambda half, c=c: v_ref.at[pl.ds(half * 256, 256), pl.ds(c * WIDTH, WIDTH)])
        for c in range(CHUNKS)
    ]

    first_block, second_block = step(y, 3 - 2 * core), step(y, 1 + 2 * core)
    stages = (
        (y, y, lambda: None),
        (first_block, second_block, u_gather.early),
        (step(y, 2), step(y, 2), u_gather.far),
        (second_block, first_block, u_gather.near),
    )

    class Piece:
        def __init__(self, s):
            self.s = s
            self.own_block, self.mate_block, self.ready = stages[s]
            self.rows = pl.multiple_of(self.own_block * 512 + core * 256, 256)
            self.reduce = Reduce(
                self.part, 128, z_ring, act_s1.at[s], act_r1.at[s], act_s2.at[s], act_r2.at[s])
            name = f"p{s}"
            steps[name + ".out"], steps[name + ".own"] = self.out, self.own
            steps[name + ".r1"], steps[name + ".r2"] = self.first, self.reduce.second
            self.gather = Gather(
                name,
                lambda p, half: act_t.at[
                    pl.ds(pl.multiple_of(self.rows + half * 128, 128), 128), at_multiple(p, 256)],
                z, z_ring, ready=self.total)
            steps[name + ".km"] = self.finish

        def inputs(self):
            landed(*act_keeps)
            a_gather.near()
            a_gather.far()
            self.ready()

        def out(self):
            self.inputs()

            @pl.loop(0, 2)
            def _(m):
                rows = at_multiple(m, 512)
                act_out[self.s, rows] = dot(a_all[rows], u_all[self.mate_block * 2 + mate]).astype(BF16)

            self.swap = send(act_out.at[self.s], act_in.at[self.s], other)

        def own(self):
            self.inputs()

            @pl.loop(0, 2)
            def _(m):
                rows = at_multiple(m, 512)
                act_part[self.s, rows] = dot(a_all[rows], u_all[self.own_block * 2 + core])

        def part(self, by):
            rows = at_multiple(step(z, by), 256)
            return act_part[self.s, rows] + act_in[self.s, rows].astype(F32)

        def first(self):
            arrive(self.swap)
            self.reduce.first()

        def total(self):
            act_t[pl.ds(self.rows, 256), at_multiple(z, 256)] = self.reduce.last().T.astype(BF16)

        def finish(self):
            self.gather.near()
            self.gather.far()
            piece = act_t.at[pl.ds(self.rows, 256)]
            self.mates = send(piece, piece, other)

        def done(self):
            self.gather.near()
            self.gather.far()
            arrive(self.mates)

    pieces = [Piece(s) for s in range(4)]

    class Chunk:
        def __init__(self, c):
            self.c = c
            self.lanes = pl.ds(c * WIDTH, WIDTH)
            self.reduce = Reduce(
                lambda by: grad_part[c, at_multiple(step(y, by), 256)], 128, y_ring,
                grad_s1.at[c], grad_r1.at[c], grad_s2.at[c], grad_r2.at[c])
            self.out = Reduce(
                self.product, 256, y_ring, tile_s1.at[c], tile_r1.at[c], tile_s2.at[c], tile_r2.at[c])
            name = f"c{c}"
            steps[name + ".mm"], steps[name + ".r2"] = self.multiply, self.reduce.second
            self.gather = Gather(
                name, lambda p, half: grad_rot.at[c, half, at_multiple(p, 128)], x, x_ring, ready=self.total)
            steps[name + ".t1"], steps[name + ".tn"] = self.out.first, self.near_tiles
            steps[name + ".t2"], steps[name + ".to"] = self.out.second, self.own_tile
            steps[name + ".fin"] = self.finish

        def multiply(self):
            g_done()
            landed(v_keeps[self.c])
            v_gathers[self.c].near()
            v_gathers[self.c].far()

            @pl.loop(0, 2)
            def _(m):
                rows = at_multiple(m, 512)
                grad_part[self.c, rows] = dot(g_all[rows], v_all[self.c])

            self.reduce.first()

        def total(self):
            total = self.reduce.last().astype(BF16)
            rows = at_multiple(x, 128)
            grad_rot[self.c, 0, rows] = total[:128]
            grad_rot[self.c, 1, rows] = total[128:]

        def tile(self, t, *needs):
            self.gather.near()
            self.gather.far()
            for piece in needs:
                piece.done()
            product = dot(act_t[at_multiple(t, 512)], grad_rot[self.c].reshape(1024, WIDTH))
            return product * product

        def product(self, by):
            if by == 2:
                return self.tile(step(y, 2), pieces[2])
            if by == 0:
                return o_ref[:, self.lanes]
            return tile_part[self.c, by // 2]

        def near_tiles(self):
            for i, by in enumerate((1, 3)):
                tile_part[self.c, i] = self.tile(step(y, by), pieces[1], pieces[3])

        def own_tile(self):
            o_ref[:, self.lanes] = self.tile(y, pieces[0])

        def finish(self):
            o_ref[:, self.lanes] = self.out.last() * (1.0 / (SEQS * SEQ_LEN))

    chunks = [Chunk(c) for c in range(CHUNKS)]
    for name in ORDER:
        steps[name]()
    for copy in sent:
        copy.wait_send()


def shards(activations, out_grads, input_basis, output_basis):
    hbm = pl.BlockSpec(memory_space=pl.ANY)
    vmem = pl.BlockSpec(memory_space=pltpu.VMEM)

    def bf16(*sizes):
        return pltpu.VMEM(sizes, BF16)

    def f32(*sizes):
        return pltpu.VMEM(sizes, F32)

    return pl.pallas_call(
        kernel,
        out_shape=jax.ShapeDtypeStruct((512, 1024), F32),
        in_specs=[hbm] * 4,
        out_specs=vmem,
        scratch_shapes=[
            bf16(1024, 1024), bf16(8, 1024, 256), bf16(1024, 2048), bf16(CHUNKS, 2048, WIDTH),
            bf16(4, 1024, 256), bf16(4, 1024, 256), f32(4, 1024, 256),
            bf16(4, 2, 128, 256), bf16(4, 2, 128, 256), bf16(4, 2, 256, 256), bf16(4, 2, 256, 256),
            bf16(2048, 1024),
            f32(CHUNKS, 1024, WIDTH),
            bf16(CHUNKS, 2, 128, WIDTH), bf16(CHUNKS, 2, 128, WIDTH),
            bf16(CHUNKS, 2, 256, WIDTH), bf16(CHUNKS, 2, 256, WIDTH), bf16(CHUNKS, 2, 512, WIDTH),
            f32(CHUNKS, 2, 512, WIDTH),
            bf16(CHUNKS, 2, 256, WIDTH), bf16(CHUNKS, 2, 256, WIDTH),
            bf16(CHUNKS, 2, 512, WIDTH), bf16(CHUNKS, 2, 512, WIDTH),
            pltpu.SemaphoreType.DMA((N_SEM,)), pltpu.SemaphoreType.DMA((N_SEM,)),
            pltpu.SemaphoreType.DMA((4 + CHUNKS,)),
        ],
        compiler_params=pltpu.CompilerParams(
            collective_id=0, has_side_effects=True, vmem_limit_bytes=60 * 2**20),
        cost_estimate=pl.CostEstimate(flops=13 * 10**9, bytes_accessed=5 * 2**20, transcendentals=0),
    )(activations, out_grads, input_basis, output_basis)


def solution(mesh):
    return jax.shard_map(
        shards,
        mesh=mesh,
        in_specs=(P("row", "col"), P("col", "row"), P("col", "row"), P("row", "col")),
        out_specs=P("row", "col"),
        check_vma=False,
    )
```

time: 353 us -> 118 us (0.33)
  waiting for transfers between devices: 304 us -> 0 us
  Pallas kernels: 0 us -> 114 us
  matrix products: 27.8 us -> 0 us
  between operations: 13.1 us -> 0.01 us
    psum x2 -> x0, waiting for transfers between devices: 203 us -> none  [the longest x1 129 us: shards(): lax.psum(grad_part, 'row').astype(jnp.float32).astype(jnp.bfloat16)]
    pallas_call x0 -> x1, Pallas kernels: none -> 114 us  [shards(): pl.pallas_call(kernel, out_shape=jax.ShapeDtypeStruct((512, 1024), F32),...]
    all_gather x2 -> x0, waiting for transfers between devices: 99.5 us -> none  [the longest x1 63.6 us: shards(): lax.all_gather(activations, 'row', axis=0, tiled=True)]
    dot_general x3 -> x0, matrix products: 27.8 us -> none  [the longest x1 9.48 us: shards(): jnp.dot(lax.all_gather(activations, 'row', axis=0, tiled=True), input_bas...]
    reshape x1 -> x0, local copies, waits for them, and re-layouts: 6.39 us -> none  [shards(): act_seqs = act_rot.reshape(SEQS, SEQ_LEN, act_rot.shape[1])]
  transfers between devices with their start and end apart: 4 -> 0, of which waited for: 4 -> 0; matrix products, arithmetic and copies ran while one was open for 7% -> 0% of each run, Pallas kernels for 0% -> 0%
where the time goes in v2:
time: 118 us; the launch traced here: 117 us
  Pallas kernels  114 us (97%)
  local copies, waits for them, and re-layouts  3.16 us (3%)
    pallas_call x1, Pallas kernels, shards(): pl.pallas_call(kernel, out_shape=jax.ShapeDtypeStruct((512, 1024), F32),...  114 us
    unnamed x1, local copies, waits for them, and re-layouts  3.16 us

profile of v2, /device:TPU:0, one launch (start us, length us, event | category | flops | bytes accessed | tf_op | source)
XLA Modules:
  0.0 117.4 jit_solution(6918509317696365824)
XLA Ops:
  0.0 114.3 %shard_map.46 = f32[512,1024]{1,0:T(8,128)} custom-call(bf16[256,1024]{1,0:T(8,128)(2,1)} %a_ref.1, bf16[512,512]{1,0:T(8,128)(2,1)} %g_ref.1, bf16[1024,512]{1,0:T(8,128)(2,1)} %u_ref.1, bf16[512,1024]{1,0:T(8,128)(2,1)} %v_ref.1), custom_call_target="tpu_custom_call" | custom-call | flops 12999999488 | bytes 5242880 | tf_op jit(solution)/shard_map/pallas_call | solution.py:393
  114.3 3.2 %copy.6 = f32[512,1024]{1,0:T(8,128)} copy(f32[512,1024]{1,0:T(8,128)} %shard_map.46) | data formatting | bytes 4194304

commit v3 on v2

--- a/solution.py
+++ b/solution.py
@@ -10,8 +10,9 @@
 MESH = pl.DeviceIdType.MESH
 BF16 = jnp.bfloat16
 F32 = jnp.float32
-CHUNKS = 4
-WIDTH = 1024 // CHUNKS
+WIDTHS = (256, 256, 256, 256)
+CHUNKS = len(WIDTHS)
+LANES = [pl.ds(sum(WIDTHS[:c]), WIDTHS[c]) for c in range(CHUNKS)]
 N_SEM = 120 + 24 * CHUNKS
 
 ORDER = (
@@ -41,7 +42,7 @@
     a_all, u_all, g_all, v_all,
     act_out, act_in, act_part, act_s1, act_r1, act_s2, act_r2, act_t,
     grad_part, grad_s1, grad_r1, grad_s2, grad_r2, grad_rot,
-    tile_part, tile_s1, tile_r1, tile_s2, tile_r2,
+    tile_part, tile_s1, tile_r1, tile_s2, tile_r2, result,
     send_sem, recv_sem, local_sem,
 ):
     row, col = lax.axis_index("row"), lax.axis_index("col")
@@ -78,7 +79,7 @@
         keep(u_ref.at[:, pl.ds(256, 256)], u_all.at[y * 2 + 1]),
     ]
     v_keeps = [
-        keep(v_ref.at[:, pl.ds(c * WIDTH, WIDTH)], v_all.at[c, at_multiple(x, 512)]) for c in range(CHUNKS)
+        keep(v_ref.at[:, lanes], v_all.at[at_multiple(x, 512), lanes]) for lanes in LANES
     ]
 
     partners = (*x_ring, *y_ring, *z_ring, x_far, other)
@@ -234,8 +235,8 @@
     v_gathers = [
         Gather(
             f"v{c}",
-            lambda p, half, c=c: v_all.at[c, pl.ds(pl.multiple_of(p * 512 + half * 256, 256), 256)], x, x_ring,
-            own=lambda half, c=c: v_ref.at[pl.ds(half * 256, 256), pl.ds(c * WIDTH, WIDTH)])
+            lambda p, half, c=c: v_all.at[pl.ds(pl.multiple_of(p * 512 + half * 256, 256), 256), LANES[c]], x, x_ring,
+            own=lambda half, c=c: v_ref.at[pl.ds(half * 256, 256), LANES[c]])
         for c in range(CHUNKS)
     ]
 
@@ -315,16 +316,16 @@
     class Chunk:
         def __init__(self, c):
             self.c = c
-            self.lanes = pl.ds(c * WIDTH, WIDTH)
+            self.lanes = lanes = LANES[c]
             self.reduce = Reduce(
-                lambda by: grad_part[c, at_multiple(step(y, by), 256)], 128, y_ring,
-                grad_s1.at[c], grad_r1.at[c], grad_s2.at[c], grad_r2.at[c])
+                lambda by: grad_part[at_multiple(step(y, by), 256), lanes], 128, y_ring,
+                *(ref.at[:, :, lanes] for ref in (grad_s1, grad_r1, grad_s2, grad_r2)))
             self.out = Reduce(
-                self.product, 256, y_ring, tile_s1.at[c], tile_r1.at[c], tile_s2.at[c], tile_r2.at[c])
+                self.product, 256, y_ring, *(ref.at[:, :, lanes] for ref in (tile_s1, tile_r1, tile_s2, tile_r2)))
             name = f"c{c}"
             steps[name + ".mm"], steps[name + ".r2"] = self.multiply, self.reduce.second
             self.gather = Gather(
-                name, lambda p, half: grad_rot.at[c, half, at_multiple(p, 128)], x, x_ring, ready=self.total)
+                name, lambda p, half: grad_rot.at[half, at_multiple(p, 128), lanes], x, x_ring, ready=self.total)
             steps[name + ".t1"], steps[name + ".tn"] = self.out.first, self.near_tiles
             steps[name + ".t2"], steps[name + ".to"] = self.out.second, self.own_tile
             steps[name + ".fin"] = self.finish
@@ -338,51 +339,58 @@
             @pl.loop(0, 2)
             def _(m):
                 rows = at_multiple(m, 512)
-                grad_part[self.c, rows] = dot(g_all[rows], v_all[self.c])
+                grad_part[rows, self.lanes] = dot(g_all[rows], v_all[:, self.lanes])
 
             self.reduce.first()
 
         def total(self):
             total = self.reduce.last().astype(BF16)
             rows = at_multiple(x, 128)
-            grad_rot[self.c, 0, rows] = total[:128]
-            grad_rot[self.c, 1, rows] = total[128:]
+            grad_rot[0, rows, self.lanes] = total[:128]
+            grad_rot[1, rows, self.lanes] = total[128:]
 
         def tile(self, t, *needs):
             self.gather.near()
             self.gather.far()
             for piece in needs:
                 piece.done()
-            product = dot(act_t[at_multiple(t, 512)], grad_rot[self.c].reshape(1024, WIDTH))
+            product = dot(act_t[at_multiple(t, 512)], grad_rot[:, :, self.lanes].reshape(1024, WIDTHS[self.c]))
             return product * product
 
         def product(self, by):
             if by == 2:
                 return self.tile(step(y, 2), pieces[2])
             if by == 0:
-                return o_ref[:, self.lanes]
-            return tile_part[self.c, by // 2]
+                return tile_part[2, :, self.lanes]
+            return tile_part[by // 2, :, self.lanes]
 
         def near_tiles(self):
             for i, by in enumerate((1, 3)):
-                tile_part[self.c, i] = self.tile(step(y, by), pieces[1], pieces[3])
+                tile_part[i, :, self.lanes] = self.tile(step(y, by), pieces[1], pieces[3])
 
         def own_tile(self):
-            o_ref[:, self.lanes] = self.tile(y, pieces[0])
+            tile_part[2, :, self.lanes] = self.tile(y, pieces[0])
 
         def finish(self):
-            o_ref[:, self.lanes] = self.out.last() * (1.0 / (SEQS * SEQ_LEN))
-
+            result[:, self.lanes] = (self.out.last() * (1.0 / (SEQS * SEQ_LEN))).astype(result.dtype)
+            results.append(keep(result.at[:, self.lanes], o_ref.at[:, self.lanes]))
+
+    results = []
     chunks = [Chunk(c) for c in range(CHUNKS)]
     for name in ORDER:
         steps[name]()
     for copy in sent:
         copy.wait_send()
+    for copy in results:
+        copy.wait()
+
+
+def hand_out(in_ref, out_ref):
+    out_ref[...] = in_ref[...]
 
 
 def shards(activations, out_grads, input_basis, output_basis):
     hbm = pl.BlockSpec(memory_space=pl.ANY)
-    vmem = pl.BlockSpec(memory_space=pltpu.VMEM)
 
     def bf16(*sizes):
         return pltpu.VMEM(sizes, BF16)
@@ -390,29 +398,33 @@
     def f32(*sizes):
         return pltpu.VMEM(sizes, F32)
 
-    return pl.pallas_call(
+    correction = pl.pallas_call(
         kernel,
         out_shape=jax.ShapeDtypeStruct((512, 1024), F32),
         in_specs=[hbm] * 4,
-        out_specs=vmem,
+        out_specs=hbm,
         scratch_shapes=[
-            bf16(1024, 1024), bf16(8, 1024, 256), bf16(1024, 2048), bf16(CHUNKS, 2048, WIDTH),
+            bf16(1024, 1024), bf16(8, 1024, 256), bf16(1024, 2048), bf16(2048, 1024),
             bf16(4, 1024, 256), bf16(4, 1024, 256), f32(4, 1024, 256),
             bf16(4, 2, 128, 256), bf16(4, 2, 128, 256), bf16(4, 2, 256, 256), bf16(4, 2, 256, 256),
             bf16(2048, 1024),
-            f32(CHUNKS, 1024, WIDTH),
-            bf16(CHUNKS, 2, 128, WIDTH), bf16(CHUNKS, 2, 128, WIDTH),
-            bf16(CHUNKS, 2, 256, WIDTH), bf16(CHUNKS, 2, 256, WIDTH), bf16(CHUNKS, 2, 512, WIDTH),
-            f32(CHUNKS, 2, 512, WIDTH),
-            bf16(CHUNKS, 2, 256, WIDTH), bf16(CHUNKS, 2, 256, WIDTH),
-            bf16(CHUNKS, 2, 512, WIDTH), bf16(CHUNKS, 2, 512, WIDTH),
+            f32(1024, 1024),
+            bf16(2, 128, 1024), bf16(2, 128, 1024), bf16(2, 256, 1024), bf16(2, 256, 1024), bf16(2, 512, 1024),
+            f32(3, 512, 1024),
+            bf16(2, 256, 1024), bf16(2, 256, 1024), bf16(2, 512, 1024), bf16(2, 512, 1024),
+            pltpu.VMEM((512, 1024), F32),
             pltpu.SemaphoreType.DMA((N_SEM,)), pltpu.SemaphoreType.DMA((N_SEM,)),
-            pltpu.SemaphoreType.DMA((4 + CHUNKS,)),
+            pltpu.SemaphoreType.DMA((4 + 2 * CHUNKS,)),
         ],
         compiler_params=pltpu.CompilerParams(
             collective_id=0, has_side_effects=True, vmem_limit_bytes=60 * 2**20),
         cost_estimate=pl.CostEstimate(flops=13 * 10**9, bytes_accessed=5 * 2**20, transcendentals=0),
     )(activations, out_grads, input_basis, output_basis)
+    half = pl.BlockSpec((256, 1024), lambda i: (i, 0))
+    return pl.pallas_call(
+        hand_out, grid=(2,), in_specs=[half], out_specs=half,
+        out_shape=jax.ShapeDtypeStruct((512, 1024), F32),
+    )(correction)
 
 
 def solution(mesh):

time: 118 us -> 116 us (0.983)
  local copies, waits for them, and re-layouts: 3.16 us -> 0 us
  Pallas kernels: 114 us -> 116 us
    unnamed x1 -> x0, local copies, waits for them, and re-layouts: 3.16 us -> none
    pallas_call x0 -> x1, Pallas kernels: none -> 2.62 us  [shards(): pl.pallas_call(hand_out, grid=(2,), in_specs=[half], out_specs=half, out_...]
where the time goes in v3:
time: 116 us
  Pallas kernels  116 us (100%)
    pallas_call x1, Pallas kernels, shards(): pl.pallas_call(kernel, out_shape=jax.ShapeDtypeStruct((512, 1024), F32),...  114 us
    pallas_call x1, Pallas kernels, shards(): pl.pallas_call(hand_out, grid=(2,), in_specs=[half], out_specs=half, out_...  2.62 us

profile of v3, /device:TPU:0, one launch (start us, length us, event | category | flops | bytes accessed | tf_op | source)
XLA Modules:
  0.0 116.2 jit_solution(10198818752522416618)
XLA Ops:
  0.0 113.6 %shard_map.46.in_ref = f32[512,1024]{1,0:T(8,128)} custom-call(bf16[256,1024]{1,0:T(8,128)(2,1)} %a_ref.1, bf16[512,512]{1,0:T(8,128)(2,1)} %g_ref.1, bf16[1024,512]{1,0:T(8,128)(2,1)} %u_ref.1, bf16[512,1024]{1,0:T(8,128)(2,1)} %v_ref.1), custom_call_target="tpu_custom_call" | custom-call | flops 12999999488 | bytes 5242880 | tf_op jit(solution)/shard_map/pallas_call | solution.py:401
  113.6 2.6 %shard_map.47 = f32[512,1024]{1,0:T(8,128)} custom-call(f32[512,1024]{1,0:T(8,128)} %shard_map.46.in_ref), custom_call_target="tpu_custom_call" | custom-call | tf_op jit(solution)/shard_map/pallas_call | solution.py:424

commit v4 on v3

--- a/solution.py
+++ b/solution.py
@@ -62,6 +62,11 @@
     x_far = device(y, step(x, 2), z, core)
     other = device(y, x, z, mate)
 
+    partners = (*x_ring, *y_ring, *z_ring, x_far, other)
+    barrier = pltpu.get_barrier_semaphore()
+    for partner in partners:
+        pl.semaphore_signal(barrier, inc=1, device_id=partner, device_id_type=MESH)
+
     local = []
 
     def keep(src, dst):
@@ -82,10 +87,6 @@
         keep(v_ref.at[:, lanes], v_all.at[at_multiple(x, 512), lanes]) for lanes in LANES
     ]
 
-    partners = (*x_ring, *y_ring, *z_ring, x_far, other)
-    barrier = pltpu.get_barrier_semaphore()
-    for partner in partners:
-        pl.semaphore_signal(barrier, inc=1, device_id=partner, device_id_type=MESH)
     pl.semaphore_wait(barrier, len(partners))
 
     sent, arrived = [], set()

time: 116 us -> 116 us (level)
  no operation moved by 1% of the time
where the time goes in v4:
time: 116 us
  Pallas kernels  116 us (100%)
    pallas_call x1, Pallas kernels, shards(): pl.pallas_call(kernel, out_shape=jax.ShapeDtypeStruct((512, 1024), F32),...  114 us
    pallas_call x1, Pallas kernels, shards(): pl.pallas_call(hand_out, grid=(2,), in_specs=[half], out_specs=half, out_...  2.62 us

profile of v4, /device:TPU:0, one launch (start us, length us, event | category | flops | bytes accessed | tf_op | source)
XLA Modules:
  0.0 116.2 jit_solution(1841542517155948971)
XLA Ops:
  0.0 113.5 %shard_map.46.in_ref = f32[512,1024]{1,0:T(8,128)} custom-call(bf16[256,1024]{1,0:T(8,128)(2,1)} %a_ref.1, bf16[512,512]{1,0:T(8,128)(2,1)} %g_ref.1, bf16[1024,512]{1,0:T(8,128)(2,1)} %u_ref.1, bf16[512,1024]{1,0:T(8,128)(2,1)} %v_ref.1), custom_call_target="tpu_custom_call" | custom-call | flops 12999999488 | bytes 5242880 | tf_op jit(solution)/shard_map/pallas_call | solution.py:402
  113.5 2.6 %shard_map.47 = f32[512,1024]{1,0:T(8,128)} custom-call(f32[512,1024]{1,0:T(8,128)} %shard_map.46.in_ref), custom_call_target="tpu_custom_call" | custom-call | tf_op jit(solution)/shard_map/pallas_call | solution.py:425
